TPU v7x, 32 devices: a whole 2x2x4 slice. The times are simulated.
32 devices in a mesh: section: 2 (over x), batch: 16 (over z, y, core).
Axes of the slice: x: 2, y: 2, z: 4, core: 2. Of those that a mesh axis runs over, the one named last changes fastest.
Arguments:
- inputs: bfloat16 [2, 16, 256, 768], P(None, 'batch'), may hold values from -6 to 6
- cotangent: bfloat16 [2, 16, 256, 768], P(None, 'batch'), may hold values from -6 to 6
- lengths: int32 [2, 16, 4], P(None, 'batch'), may hold values from 1 to 128, 256 in all within a row
- qkv_weight: bfloat16 [2, 768, 2304], P('section', 'batch'), may hold values from -0.21875 to 0.21875
- out_weight: bfloat16 [2, 768, 768], P('section', 'batch'), may hold values from -0.875 to 0.875
- up_weight: bfloat16 [2, 768, 3072], P('section', 'batch'), may hold values from -0.21875 to 0.21875
- down_weight: bfloat16 [2, 3072, 768], P('section', 'batch'), may hold values from -0.109375 to 0.109375
- biases: bfloat16 [2, 6144], P('section', 'batch'), may hold values from -3 to 3
- norm_gains: bfloat16 [2, 2, 768], P('section', None, 'batch'), may hold values from 0.099609375 to 1.8984375
- norm_shifts: bfloat16 [2, 2, 768], P('section', None, 'batch'), may hold values from -3 to 3
Outputs:
- activations: bfloat16 [2, 2, 16, 256, 768], P('section', None, 'batch')
- input_grads: bfloat16 [2, 2, 16, 256, 768], P('section', None, 'batch')
- qkv_grad: float32 [2, 768, 2304], P('section', 'batch')
- out_grad: float32 [2, 768, 768], P('section', 'batch')
- up_grad: float32 [2, 768, 3072], P('section', 'batch')
- down_grad: float32 [2, 3072, 768], P('section', 'batch')
- bias_grad: float32 [2, 6144], P('section', 'batch')
- gain_grad: float32 [2, 2, 768], P('section', None, 'batch')
- shift_grad: float32 [2, 2, 768], P('section', None, 'batch')
Inputs may be any that keep to these rules, and one draw needn't show every extreme that they name: In each packed row the 4 lengths sum to 256, and one of them equals 128.
All inputs are finite; a program needn't handle non-finite values.
Results may differ from a plain program's by a relative error of at most 0.025.
Values may be sent and summed in bfloat16 or wider, within the bound.
No kernel may reach another device: no remote copies, remote signals or barrier semaphores. Data moves between devices by JAX's collectives and lax.ppermute only.
A program may use at most 192 MiB of HBM per device.

v0:
```python
from functools import partial

import jax
import jax.numpy as jnp
from jax import lax
from jax.sharding import PartitionSpec as P

D = 768
HEADS = 12
FF = 3072
HEAD_DIM = 64
ROW = 256


epsilon = 1e-12
masked_value = -1e30


def from_behind(value, axis, steps):
    count = lax.axis_size(axis)
    first, last = (max(0, -steps), min(count, count - steps))
    return lax.ppermute(value, axis, [(source, source + steps) for source in range(first, last)])


def layer_norm(values, gain_vec, shift_vec):
    average = jnp.mean(values, axis=-1, keepdims=True)
    centred = values - average
    spread = jnp.mean(centred * centred, axis=-1, keepdims=True)
    return centred * lax.rsqrt(spread + epsilon) * gain_vec + shift_vec


def segment_masks(row_lengths):
    bounds = jnp.cumsum(row_lengths, axis=-1)
    places = jnp.arange(ROW, dtype=jnp.int32)
    segment = jnp.sum((places[None, :, None] >= bounds[:, None, :]).astype(jnp.int32), axis=-1)
    return segment[:, :, None] == segment[:, None, :]


def attention_scores(queries, key_rows, row_masks):
    raw_scores = jnp.einsum(
        "rqhd,rkhd->rhqk", queries, key_rows, preferred_element_type=jnp.float32
    )
    return jnp.where(row_masks[:, None], raw_scores * HEAD_DIM ** (-0.5), masked_value)


def small_vectors(weights):
    return (
        weights[4].astype(jnp.float32),
        weights[5].astype(jnp.float32),
        weights[6].astype(jnp.float32),
    )


def layer_forward(tokens, row_masks, weights):
    qkv_w, out_w, up_w, down_w = (weights[0], weights[1], weights[2], weights[3])
    bias_vec, gain_pair, shift_pair = small_vectors(weights)
    rows_here = tokens.shape[0]
    shaped = (rows_here, ROW, HEADS, HEAD_DIM)
    flat_tokens = tokens.reshape(rows_here * ROW, D)
    joined_proj = jnp.dot(flat_tokens, qkv_w, preferred_element_type=jnp.float32)
    queries = (joined_proj[:, :D] + bias_vec[:D]).astype(jnp.bfloat16).reshape(shaped)
    key_rows = joined_proj[:, D : 2 * D].astype(jnp.bfloat16).reshape(shaped)
    value_rows = (
        (joined_proj[:, 2 * D :] + bias_vec[D : 2 * D]).astype(jnp.bfloat16).reshape(shaped)
    )
    raw_scores = attention_scores(queries, key_rows, row_masks)
    row_peak = jnp.max(raw_scores, axis=-1, keepdims=True)
    exp_scores = jnp.exp(raw_scores - row_peak)
    row_total = jnp.sum(exp_scores, axis=-1, keepdims=True)
    attn_probs = (exp_scores / row_total).astype(jnp.bfloat16)
    log_total = row_peak + jnp.log(row_total)
    context = jnp.einsum(
        "rhqk,rkhd->rqhd", attn_probs, value_rows, preferred_element_type=jnp.float32
    )
    context = context.reshape(rows_here * ROW, D).astype(jnp.bfloat16)
    attended = jnp.dot(context, out_w, preferred_element_type=jnp.float32) + bias_vec[2 * D : 3 * D]
    first_sum = flat_tokens.astype(jnp.float32) + attended
    normed = layer_norm(first_sum, gain_pair[0], shift_pair[0])
    hidden = normed.astype(jnp.bfloat16)
    inner_pre = (
        jnp.dot(hidden, up_w, preferred_element_type=jnp.float32) + bias_vec[3 * D : 3 * D + FF]
    )
    active = jax.nn.gelu(inner_pre, approximate=False).astype(jnp.bfloat16)
    second_sum = (
        normed
        + jnp.dot(active, down_w, preferred_element_type=jnp.float32)
        + bias_vec[3 * D + FF :]
    )
    result = (
        layer_norm(second_sum, gain_pair[1], shift_pair[1])
        .astype(jnp.bfloat16)
        .reshape(tokens.shape)
    )
    kept_state = (
        flat_tokens,
        queries,
        key_rows,
        value_rows,
        log_total,
        context,
        first_sum,
        hidden,
        inner_pre,
        second_sum,
    )
    return (result, kept_state)


def blank_forward(operand):
    tokens = operand[0]
    rows_here = tokens.shape[0]
    token_count = rows_here * ROW
    shaped = (rows_here, ROW, HEADS, HEAD_DIM)
    kept_state = (
        jnp.zeros((token_count, D), jnp.bfloat16),
        jnp.zeros(shaped, jnp.bfloat16),
        jnp.zeros(shaped, jnp.bfloat16),
        jnp.zeros(shaped, jnp.bfloat16),
        jnp.zeros((rows_here, HEADS, ROW, 1), jnp.float32),
        jnp.zeros((token_count, D), jnp.bfloat16),
        jnp.zeros((token_count, D), jnp.float32),
        jnp.zeros((token_count, D), jnp.bfloat16),
        jnp.zeros((token_count, FF), jnp.float32),
        jnp.zeros((token_count, D), jnp.float32),
    )
    return (jnp.zeros_like(tokens), kept_state)


def ffn_backward(kept_state, out_grad, weights):
    up_w, down_w = (weights[2], weights[3])
    bias_vec, gain_pair, shift_pair = small_vectors(weights)
    hidden, inner_pre, second_sum = (kept_state[7], kept_state[8], kept_state[9])
    normed_out, norm_back = jax.vjp(layer_norm, second_sum, gain_pair[1], shift_pair[1])
    sum_grad, gain_grad, shift_grad = norm_back(out_grad)
    branch_grad = sum_grad.astype(jnp.bfloat16)
    gelu_value, gelu_back = jax.vjp(partial(jax.nn.gelu, approximate=False), inner_pre)
    active = gelu_value.astype(jnp.bfloat16)
    through = jnp.einsum("nd,fd->nf", branch_grad, down_w, preferred_element_type=jnp.float32)
    inner_grad = gelu_back(through)[0].astype(jnp.bfloat16)
    hidden_grad = sum_grad + jnp.einsum(
        "nf,df->nd", inner_grad, up_w, preferred_element_type=jnp.float32
    )
    small_terms = (
        jnp.sum(inner_grad.astype(jnp.float32), axis=0),
        jnp.sum(branch_grad.astype(jnp.float32), axis=0),
        gain_grad,
        shift_grad,
    )
    ffn_parts = (hidden, inner_grad, active, branch_grad)
    return (hidden_grad, small_terms, ffn_parts)


def ffn_weights(ffn_parts):
    hidden, inner_grad, active, branch_grad = ffn_parts
    up_grad = jnp.einsum("nd,nf->df", hidden, inner_grad, preferred_element_type=jnp.float32)
    down_grad = jnp.einsum("nf,nd->fd", active, branch_grad, preferred_element_type=jnp.float32)
    return (up_grad, down_grad)


def blank_ffn(deferred, operand):
    token_count = operand[1].shape[0]
    small_terms = (
        jnp.zeros((FF,), jnp.float32),
        jnp.zeros((D,), jnp.float32),
        jnp.zeros((D,), jnp.float32),
        jnp.zeros((D,), jnp.float32),
    )
    extra = (
        jnp.zeros((token_count, D), jnp.bfloat16),
        jnp.zeros((token_count, FF), jnp.bfloat16),
        jnp.zeros((token_count, FF), jnp.bfloat16),
        jnp.zeros((token_count, D), jnp.bfloat16),
    )
    return (jnp.zeros((token_count, D), jnp.float32), small_terms, extra)


def attention_backward(kept_state, hidden_grad, row_masks, weights):
    qkv_w, out_w = (weights[0], weights[1])
    bias_vec, gain_pair, shift_pair = small_vectors(weights)
    flat_tokens, queries, key_rows, value_rows, log_total, context, first_sum = kept_state[:7]
    normed_out, norm_back = jax.vjp(layer_norm, first_sum, gain_pair[0], shift_pair[0])
    sum_grad, gain_grad, shift_grad = norm_back(hidden_grad)
    attended_grad = sum_grad.astype(jnp.bfloat16)
    context_grad = (
        jnp.einsum("ne,de->nd", attended_grad, out_w, preferred_element_type=jnp.float32)
        .astype(jnp.bfloat16)
        .reshape(queries.shape)
    )
    attn_probs = jnp.exp(attention_scores(queries, key_rows, row_masks) - log_total)
    prob_grad = jnp.einsum(
        "rqhd,rkhd->rhqk", context_grad, value_rows, preferred_element_type=jnp.float32
    )
    inner_sum = jnp.sum(attn_probs * prob_grad, axis=-1, keepdims=True)
    score_grad = (attn_probs * (prob_grad - inner_sum) * HEAD_DIM ** (-0.5)).astype(jnp.bfloat16)
    query_grad = jnp.einsum(
        "rhqk,rkhd->rqhd", score_grad, key_rows, preferred_element_type=jnp.float32
    ).astype(jnp.bfloat16)
    key_grad = jnp.einsum(
        "rhqk,rqhd->rkhd", score_grad, queries, preferred_element_type=jnp.float32
    ).astype(jnp.bfloat16)
    value_grad = jnp.einsum(
        "rhqk,rqhd->rkhd",
        attn_probs.astype(jnp.bfloat16),
        context_grad,
        preferred_element_type=jnp.float32,
    ).astype(jnp.bfloat16)
    flat_shape = (flat_tokens.shape[0], D)
    joined_grad = jnp.concatenate(
        [
            query_grad.reshape(flat_shape),
            key_grad.reshape(flat_shape),
            value_grad.reshape(flat_shape),
        ],
        axis=1,
    )
    input_grad = sum_grad + jnp.einsum(
        "ne,de->nd", joined_grad, qkv_w, preferred_element_type=jnp.float32
    )
    small_terms = (
        jnp.sum(joined_grad[:, :D].astype(jnp.float32), axis=0),
        jnp.sum(joined_grad[:, 2 * D :].astype(jnp.float32), axis=0),
        jnp.sum(attended_grad.astype(jnp.float32), axis=0),
        gain_grad,
        shift_grad,
    )
    attn_parts = (flat_tokens, joined_grad, context, attended_grad)
    return (input_grad, small_terms, attn_parts)


def attention_weights(attn_parts):
    flat_tokens, joined_grad, context, attended_grad = attn_parts
    qkv_grad = jnp.einsum("nd,ne->de", flat_tokens, joined_grad, preferred_element_type=jnp.float32)
    out_grad = jnp.einsum("nd,ne->de", context, attended_grad, preferred_element_type=jnp.float32)
    return (qkv_grad, out_grad)


def blank_attention(deferred, operand):
    token_count = operand[1].shape[0]
    small_terms = tuple((jnp.zeros((D,), jnp.float32) for index in range(5)))
    extra = (
        jnp.zeros((token_count, D), jnp.bfloat16),
        jnp.zeros((token_count, 3 * D), jnp.bfloat16),
        jnp.zeros((token_count, D), jnp.bfloat16),
        jnp.zeros((token_count, D), jnp.bfloat16),
    )
    return (jnp.zeros((token_count, D), jnp.float32), small_terms, extra)


def add_tuples(first, second):
    return second if first is None else tuple(map(jnp.add, first, second))


def body(
    inputs,
    cotangent,
    lengths,
    qkv_weight,
    out_weight,
    up_weight,
    down_weight,
    biases,
    norm_gains,
    norm_shifts,
):
    gathered = (
        lax.all_gather(qkv_weight, "batch", axis=1, tiled=True),
        lax.all_gather(out_weight, "batch", axis=1, tiled=True),
        lax.all_gather(up_weight, "batch", axis=1, tiled=True),
        lax.all_gather(down_weight, "batch", axis=1, tiled=True),
        lax.all_gather(biases, "batch", axis=1, tiled=True),
        lax.all_gather(norm_gains, "batch", axis=2, tiled=True),
        lax.all_gather(norm_shifts, "batch", axis=2, tiled=True),
    )
    weights = tuple((member[0] for member in gathered))
    first_section = lax.axis_index("section") == 0
    later_section = jnp.logical_not(first_section)
    micro_count = inputs.shape[0]
    row_masks = [segment_masks(lengths[micro_index]) for micro_index in range(micro_count)]

    def run_forward(operand):
        return layer_forward(operand[0], operand[1], weights)

    def run_ffn(operand):
        hidden_grad, small_terms, ffn_parts = ffn_backward(operand[0], operand[1], weights)
        return (hidden_grad, small_terms, ffn_parts)

    def run_attention(operand):
        input_grad, small_terms, attn_parts = attention_backward(
            operand[0], operand[1], operand[2], weights
        )
        return (input_grad, small_terms, attn_parts)

    received = inputs[0]
    outputs_steps = []
    kept_steps = []
    for step_index in range(micro_count + 1):
        if step_index == 0:
            operand = (inputs[0], row_masks[0])
            result, kept_state = lax.cond(first_section, run_forward, blank_forward, operand)
        elif step_index == micro_count:
            operand = (received, row_masks[step_index - 1])
            result, kept_state = lax.cond(later_section, run_forward, blank_forward, operand)
        else:
            operand = (
                jnp.where(first_section, inputs[step_index], received),
                jnp.where(first_section, row_masks[step_index], row_masks[step_index - 1]),
            )
            result, kept_state = run_forward(operand)
        outputs_steps.append(result)
        kept_steps.append((kept_state, operand[1]))
        if step_index < micro_count:
            received = from_behind(result, "section", 1)
    ffn_small = None
    attn_small = None
    ffn_mats = None
    attn_mats = None
    ffn_summed = None
    ffn_list = []
    attn_list = []
    sent_back = cotangent[0]
    grads_steps = []
    for back_index in range(micro_count + 1):
        kept_state, mask_now = kept_steps[micro_count - back_index]
        edge_step = back_index == 0 or back_index == micro_count
        if back_index == 0:
            grad_out = cotangent[micro_count - 1]
            valid_now = later_section
        elif back_index == micro_count:
            grad_out = sent_back
            valid_now = first_section
        else:
            grad_out = jnp.where(first_section, sent_back, cotangent[micro_count - 1 - back_index])
            valid_now = first_section
        grad_out = grad_out.reshape(-1, D).astype(jnp.float32)
        if edge_step:
            hidden_grad, small_terms, ffn_extra = lax.cond(
                valid_now, run_ffn, partial(blank_ffn, True), (kept_state, grad_out)
            )
        else:
            hidden_grad, small_terms, ffn_extra = run_ffn((kept_state, grad_out))
        ffn_small = add_tuples(ffn_small, small_terms)
        ffn_list.append(ffn_extra)
        if edge_step:
            input_grad, small_terms, attn_extra = lax.cond(
                valid_now,
                run_attention,
                partial(blank_attention, True),
                (kept_state, hidden_grad, mask_now),
            )
        else:
            input_grad, small_terms, attn_extra = run_attention((kept_state, hidden_grad, mask_now))
        attn_small = add_tuples(attn_small, small_terms)
        attn_list.append(attn_extra)
        input_low = input_grad.astype(jnp.bfloat16).reshape(cotangent.shape[1:])
        grads_steps.append(input_low)
        if back_index < micro_count:
            sent_back = from_behind(input_low, "section", -1)
    for ffn_parts in ffn_list:
        ffn_mats = add_tuples(ffn_mats, ffn_weights(ffn_parts))
    ffn_summed = ffn_mats
    for attn_parts in attn_list:
        attn_mats = add_tuples(attn_mats, attention_weights(attn_parts))
    bias_total = jnp.concatenate(
        [attn_small[0], attn_small[1], attn_small[2], ffn_small[0], ffn_small[1]]
    )
    gain_total = jnp.stack([attn_small[3], ffn_small[2]])
    shift_total = jnp.stack([attn_small[4], ffn_small[3]])
    qkv_sum, out_sum, up_sum, down_sum, bias_sum, gain_sum, shift_sum = (
        lax.psum_scatter(attn_mats[0][None], "batch", scatter_dimension=1, tiled=True),
        lax.psum_scatter(attn_mats[1][None], "batch", scatter_dimension=1, tiled=True),
        lax.psum_scatter(ffn_summed[0][None], "batch", scatter_dimension=1, tiled=True),
        lax.psum_scatter(ffn_summed[1][None], "batch", scatter_dimension=1, tiled=True),
        lax.psum_scatter(bias_total[None], "batch", scatter_dimension=1, tiled=True),
        lax.psum_scatter(gain_total[None], "batch", scatter_dimension=2, tiled=True),
        lax.psum_scatter(shift_total[None], "batch", scatter_dimension=2, tiled=True),
    )
    activations = jnp.stack(
        [
            jnp.where(first_section, outputs_steps[micro_index], outputs_steps[micro_index + 1])
            for micro_index in range(micro_count)
        ]
    )[None]
    input_grads = jnp.stack(
        [
            jnp.where(
                first_section,
                grads_steps[micro_count - micro_index],
                grads_steps[micro_count - 1 - micro_index],
            )
            for micro_index in range(micro_count)
        ]
    )[None]
    return (
        activations,
        input_grads,
        qkv_sum,
        out_sum,
        up_sum,
        down_sum,
        bias_sum,
        gain_sum,
        shift_sum,
    )


def solution(mesh):
    in_specs = (
        P(None, "batch", None, None),
        P(None, "batch", None, None),
        P(None, "batch", None),
        P("section", "batch", None),
        P("section", "batch", None),
        P("section", "batch", None),
        P("section", "batch", None),
        P("section", "batch"),
        P("section", None, "batch"),
        P("section", None, "batch"),
    )
    out_specs = (
        P("section", None, "batch", None, None),
        P("section", None, "batch", None, None),
        P("section", "batch", None),
        P("section", "batch", None),
        P("section", "batch", None),
        P("section", "batch", None),
        P("section", "batch"),
        P("section", None, "batch"),
        P("section", None, "batch"),
    )
    return jax.shard_map(body, mesh=mesh, in_specs=in_specs, out_specs=out_specs, check_vma=False)
```

profile of v0, /device:TPU:0, one launch (start us, length us, event | category | flops | bytes accessed | tf_op | source)
XLA Modules:
  0.0 1117.6 jit_solution(3284271525909719078)
XLA Ops:
  11.8 25.0 %all_gather.24 = bf16[1,2,768]{1,0,2:T(2,128)(2,1)S(1)} all-gather(bf16[1,2,48]{1,0,2:T(2,128)(2,1)S(1)} %copy.207), channel_id=1, replica_groups=mesh['section'=2,'batch'=16] {'batch'}, dimensions={2}, use_global_device_ids=true | all-gather | bytes 3264 | tf_op jit(solution)/shard_map/all_gather | solution.py:271
  37.9 18.7 %all_gather.25 = bf16[1,2,768]{1,0,2:T(2,128)(2,1)S(1)} all-gather(bf16[1,2,48]{1,0,2:T(2,128)(2,1)S(1)} %copy.209), channel_id=1, replica_groups=mesh['section'=2,'batch'=16] {'batch'}, dimensions={2}, use_global_device_ids=true | all-gather | bytes 3264 | tf_op jit(solution)/shard_map/all_gather | solution.py:272
  56.8 19.2 %all_gather.22 = bf16[1,6144]{1,0:T(2,128)(2,1)S(1)} all-gather(bf16[1,384]{1,0:T(2,128)(2,1)} %param.29), channel_id=1, replica_groups=mesh['section'=2,'batch'=16] {'batch'}, dimensions={1}, use_global_device_ids=true | all-gather | bytes 13056 | tf_op jit(solution)/shard_map/all_gather | solution.py:270
  78.1 23.1 %all-gather.5.cloned.1.call-done = bf16[1,768,2304]{2,1,0:T(8,128)(2,1)} async-done(((bf16[1,48,2304]{2,1,0:T(8,128)(2,1)}), bf16[1,768,2304]{2,1,0:T(8,128)(2,1)}) %all-gather.5.cloned.1.call-update) | async-done | bytes 3538960 | tf_op jit(solution)/shard_map/all_gather | solution.py:266
  101.2 54.7 %all-gather.9.cloned.1.call-done = bf16[1,768,3072]{2,1,0:T(8,128)(2,1)} async-done(((bf16[1,48,3072]{2,1,0:T(8,128)(2,1)}), bf16[1,768,3072]{2,1,0:T(8,128)(2,1)}) %all-gather.9.cloned.1.call-update) | async-done | bytes 4718608 | tf_op jit(solution)/shard_map/all_gather | solution.py:268
  155.9 54.1 %all-gather.11.cloned.1.call-done = bf16[1,3072,768]{2,1,0:T(8,128)(2,1)} async-done(((bf16[1,192,768]{2,1,0:T(8,128)(2,1)}), bf16[1,3072,768]{2,1,0:T(8,128)(2,1)}) %all-gather.11.cloned.1.call-update) | async-done | bytes 4718608 | tf_op jit(solution)/shard_map/all_gather | solution.py:269
  210.1 35.7 %conditional.6 = (bf16[1,256,768]{2,1,0:T(8,128)(2,1)S(1)}, bf16[256,768]{1,0:T(8,128)(2,1)}, bf16[1,256,12,64]{1,3,2,0:T(8,128)(2,1)}, bf16[1,256,12,64]{1,3,2,...) conditional(s32[]{:T(128)} %convert_element_type.416, () %tuple.58, ...), branch_computations={%region_2.3_spmd, %region_3.10_spmd} | conditional | flops 3892838912 | bytes 85172656 | solution.py:299
  232.6 10.4 fusion.301
  249.7 6.5 collective-permute-done
  265.8 11.1 multiply_convert_fusion.5
  286.3 6.8 collective-permute-done.1
  293.1 9.1 conditional.7
  302.9 8.3 conditional.8
  311.8 6.1 conditional.9
  321.2 96.0 %collective-permute-done.2 = bf16[1,256,768]{2,1,0:T(8,128)(2,1)S(1)} collective-permute-done((bf16[1,256,768]{2,1,0:T(8,128)(2,1)}, bf16[1,256,768]{2,1,0:T(8,128)(2,1)S(1)}, u32[]{:S(2)}, u32[]{:S(2)}) %collective-permute-start.2) | collective-permute-done | bytes 393248 | tf_op jit(solution)/shard_map/ppermute | solution.py:22
  423.1 6.6 convert_reduce_fusion.16
  437.1 6.9 fusion.251
  444.0 7.4 convert_reduce_fusion.21
  466.1 27.3 %conditional.10 = (f32[256,768]{1,0:T(8,128)S(1)}, f32[3072]{0:T(1024)}, f32[768]{0:T(1024)S(1)}, f32[768]{0:T(1024)}, f32[768]{0:T(1024)S(1)}, /*index=5*/bf16[...) conditional(s32[]{:T(128)} %convert_element_type.416, () %tuple.63, ...), branch_computations={%region_53.54_spmd, %region_54.63_spmd} | conditional | flops 2485122304 | bytes 64934608 | solution.py:336
  466.3 8.9 multiply_convert_fusion.2
  482.5 7.8 convert_reduce_fusion.8
  495.2 39.8 %conditional.11 = (f32[768]{0:T(1024)}, f32[768]{0:T(1024)}, f32[768]{0:T(1024)}, f32[768]{0:T(1024)}, f32[768]{0:T(1024)}, /*index=5*/bf16[256,768]{1,0:T(8,128...) conditional(s32[]{:T(128)} %convert_element_type.416, () %tuple.62, ...), branch_computations={%region_63.64_spmd, %region_64.75_spmd} | conditional | flops 1732515072 | bytes 74455720 | solution.py:344
  513.6 4.7 convert_reduce_fusion.14
  521.0 6.4 fusion.200
  568.1 6.6 add_bitcast_fusion.3
  579.3 6.1 add_bitcast_fusion.2
  592.3 57.0 %reduce-scatter.26.cloned.1.call-done = f32[48,2]{1,0:T(8,128)} async-done(((f32[768,2]{1,0:T(8,128)}), f32[48,2]{1,0:T(8,128)}) %reduce-scatter.26.cloned.1.call-update) | async-done | bytes 400
  650.7 67.7 %reduce-scatter.22.cloned.1.call-done = f32[384,1]{1,0:T(8,128)} async-done(((f32[6144,1]{1,0:T(8,128)}), f32[384,1]{1,0:T(8,128)}) %reduce-scatter.22.cloned.1.call-update) | async-done | bytes 1552
  720.0 64.7 %reduce-scatter.16.cloned.1.call-done = f32[1,48,768]{2,1,0:T(8,128)} async-done(((f32[1,768,768]{2,1,0:T(8,128)}), f32[1,48,768]{2,1,0:T(8,128)}) %reduce-scatter.16.cloned.1.call-update) | async-done | bytes 147472 | tf_op jit(solution)/shard_map/reduce_scatter | solution.py:370
  784.7 94.2 %reduce-scatter.14.cloned.1.call-done = f32[1,48,2304]{2,1,0:T(8,128)} async-done(((f32[1,768,2304]{2,1,0:T(8,128)}), f32[1,48,2304]{2,1,0:T(8,128)}) %reduce-scatter.14.cloned.1.call-update) | async-done | bytes 442384 | tf_op jit(solution)/shard_map/reduce_scatter | solution.py:369
  878.9 115.4 %reduce-scatter.18.cloned.1.call-done = f32[1,48,3072]{2,1,0:T(8,128)} async-done(((f32[1,768,3072]{2,1,0:T(8,128)}), f32[1,48,3072]{2,1,0:T(8,128)}) %reduce-scatter.18.cloned.1.call-update) | async-done | bytes 589840 | tf_op jit(solution)/shard_map/reduce_scatter | solution.py:371
  994.3 116.4 %reduce-scatter.20.cloned.1.call-done = f32[1,192,768]{2,1,0:T(8,128)} async-done(((f32[1,3072,768]{2,1,0:T(8,128)}), f32[1,192,768]{2,1,0:T(8,128)}) %reduce-scatter.20.cloned.1.call-update) | async-done | bytes 589840 | tf_op jit(solution)/shard_map/reduce_scatter | solution.py:372
  (418 shorter events, 195.8 us)
Async XLA Ops:
  7.2 71.0 %all-gather.7.cloned.1.call-start = ((), (), s32[]{:S(2)}) async-start(), calls=%async_computation.8 | async-start | bytes 1253376 | tf_op jit(solution)/shard_map/all_gather | solution.py:267
  7.9 93.3 %all-gather.5.cloned.1.call-start = ((), (), s32[]{:S(2)}) async-start(), calls=%async_computation.7 | async-start | bytes 3760128 | tf_op jit(solution)/shard_map/all_gather | solution.py:266
  8.7 147.3 %all-gather.9.cloned.1.call-start = ((), (), s32[]{:S(2)}) async-start(), calls=%async_computation.9 | async-start | bytes 5013504 | tf_op jit(solution)/shard_map/all_gather | solution.py:268
  9.4 200.6 %all-gather.11.cloned.1.call-start = ((), (), s32[]{:S(2)}) async-start(), calls=%async_computation.10 | async-start | bytes 5013504 | tf_op jit(solution)/shard_map/all_gather | solution.py:269
  10.0 580.9 %reduce-scatter.24.cloned.1.call-start = ((), (), s32[]{:S(2)}) async-start(), calls=%async_computation.16 | async-start | bytes 417792
  56.8 153.2 %copy-start.63 = (bf16[1,2,768]{2,1,0:T(2,128)(2,1)}, bf16[1,2,768]{2,1,0:T(2,128)(2,1)S(1)}, u32[]{:S(2)}) copy-start(bf16[1,2,768]{2,1,0:T(2,128)(2,1)S(1)} %copy.210) | copy-start | bytes 9220
  76.8 133.3 %copy-start.69 = (s32[256]{0:T(256)}, s32[256]{0:T(256)S(1)}, u32[]{:S(2)}) copy-start(s32[256]{0:T(256)S(1)} %get-tuple-element.738) | copy-start | bytes 3076
  78.1 131.9 %copy-start.46 = (pred[1,256,256]{1,2,0:T(8,128)(4,1)}, pred[1,256,256]{1,2,0:T(8,128)(4,1)S(1)}, u32[]{:S(2)}) copy-start(pred[1,256,256]{1,2,0:T(8,128)(4,1)S(1)} %broadcast_compare_fusion.1) | copy-start | bytes 196612
  245.8 14.7 %copy-start.81 = (f32[1,12,256,1]{2,1,3,0:T(8,128)}, f32[1,12,256,1]{2,1,3,0:T(8,128)S(1)}, u32[]{:S(2)}) copy-start(f32[1,12,256,1]{2,1,3,0:T(8,128)S(1)} %get-tuple-element.248) | copy-start | bytes 36868
  245.8 10.4 collective-permute-start
  248.8 28.2 %copy-start.54 = (f32[768]{0:T(1024)}, f32[768]{0:T(1024)S(1)}, u32[]{:S(2)}) copy-start(f32[768]{0:T(1024)S(1)} %get-tuple-element.739) | copy-start | bytes 9220
  248.8 28.2 %copy-start.57 = (f32[768]{0:T(1024)}, f32[768]{0:T(1024)S(1)}, u32[]{:S(2)}) copy-start(f32[768]{0:T(1024)S(1)} %get-tuple-element.638) | copy-start | bytes 9220
  264.4 12.6 %slice-start.12 = ((s8[4718592]{0:T(1024)(128)(4,1)}), s8[4194304]{0:T(1024)(128)(4,1)S(1)}, s32[]{:S(2)}) async-start(s8[4718592]{0:T(1024)(128)(4,1)} %bitcast.454), calls=%async_computation.30 | async-start | bytes 8388608
  265.0 167.0 %copy-start.5 = (f32[256,768]{1,0:T(8,128)}, f32[256,768]{1,0:T(8,128)S(1)}, u32[]{:S(2)}) copy-start(f32[256,768]{1,0:T(8,128)S(1)} %get-tuple-element.726) | copy-start | bytes 2359300
  265.0 12.0 %copy-start.70 = (f32[256]{0:T(256)}, f32[256]{0:T(256)S(1)}, u32[]{:S(2)}) copy-start(f32[256]{0:T(256)S(1)} %broadcast_multiply_fusion.9) | copy-start | bytes 3076
  280.4 12.7 %copy-start.32 = (bf16[1,256,768]{2,1,0:T(8,128)(2,1)}, bf16[1,256,768]{2,1,0:T(8,128)(2,1)S(1)}, u32[]{:S(2)}) copy-start(bf16[1,256,768]{2,1,0:T(8,128)(2,1)S(1)} %get-tuple-element.674) | copy-start | bytes 1179652
  280.4 12.7 %collective-permute-start.1 = (bf16[1,256,768]{2,1,0:T(8,128)(2,1)S(1)}, bf16[1,256,768]{2,1,0:T(8,128)(2,1)S(1)}, u32[]{:S(2)}, u32[]{:S(2)}) collective-permute-start(bf16[1,256,768]{2,1,0:T(8,128)(2,1)S(1)} %get-tuple-element.674), channel_id=1, source_target_pairs={{0,16},{1,17},{2,18},{3,19},{4,20},{5,21},{6,22},{7,23},{8,24},{9,... | collective-permute-start | bytes 1179656 | tf_op jit(solution)/shard_map/ppermute | solution.py:22
  311.8 107.1 %copy-start.60 = (f32[768]{0:T(1024)S(1)}, f32[768]{0:T(1024)}, u32[]{:S(2)}) copy-start(f32[768]{0:T(1024)} %get-tuple-element.740) | copy-start | bytes 9220
  317.8 105.2 %copy-start.84 = (f32[768]{0:T(1024)}, f32[768]{0:T(1024)S(1)}, u32[]{:S(2)}) copy-start(f32[768]{0:T(1024)S(1)} %get-tuple-element.286) | copy-start | bytes 9220
  317.8 111.8 %copy-start.86 = (f32[768]{0:T(1024)}, f32[768]{0:T(1024)S(1)}, u32[]{:S(2)}) copy-start(f32[768]{0:T(1024)S(1)} %get-tuple-element.288) | copy-start | bytes 9220
  317.8 99.4 %collective-permute-start.2 = (bf16[1,256,768]{2,1,0:T(8,128)(2,1)}, bf16[1,256,768]{2,1,0:T(8,128)(2,1)S(1)}, u32[]{:S(2)}, u32[]{:S(2)}) collective-permute-start(bf16[1,256,768]{2,1,0:T(8,128)(2,1)} %bitcast.91), channel_id=1, source_target_pairs={{16,0},{17,1},{18,2},{19,3},{20,4},{21,5},{22,6},{23,7},{24,8},{25... | collective-permute-start | bytes 1179656 | tf_op jit(solution)/shard_map/ppermute | solution.py:22
  319.7 103.4 %copy-start.102 = (f32[256,3072]{1,0:T(8,128)S(1)}, f32[256,3072]{1,0:T(8,128)}, u32[]{:S(2)}) copy-start(f32[256,3072]{1,0:T(8,128)} %get-tuple-element.676) | copy-start | bytes 9437188
  437.0 14.4 %copy-start.44 = (bf16[12,64,256]{2,1,0:T(8,128)(2,1)}, bf16[12,64,256]{2,1,0:T(8,128)(2,1)S(1)}, u32[]{:S(2)}) copy-start(bf16[12,64,256]{2,1,0:T(8,128)(2,1)S(1)} %get-tuple-element.734) | copy-start | bytes 1179652
  454.8 11.3 %collective-permute-start.3 = (bf16[1,256,768]{2,1,0:T(8,128)(2,1)S(1)}, bf16[1,256,768]{2,1,0:T(8,128)(2,1)S(1)}, u32[]{:S(2)}, u32[]{:S(2)}) collective-permute-start(bf16[1,256,768]{2,1,0:T(8,128)(2,1)S(1)} %bitcast.413), channel_id=1, source_target_pairs={{16,0},{17,1},{18,2},{19,3},{20,4},{21,5},{22,6},{23,7},{24,8},{25... | collective-permute-start | bytes 1179656 | tf_op jit(solution)/shard_map/ppermute | solution.py:22
  466.1 27.9 %copy-start.75 = (f32[768]{0:T(1024)S(1)}, f32[768]{0:T(1024)}, u32[]{:S(2)}) copy-start(f32[768]{0:T(1024)} %get-tuple-element.632) | copy-start | bytes 9220
  466.2 13.8 %copy-start.13 = (bf16[1,256,768]{2,1,0:T(8,128)(2,1)}, bf16[1,256,768]{2,1,0:T(8,128)(2,1)S(1)}, u32[]{:S(2)}) copy-start(bf16[1,256,768]{2,1,0:T(8,128)(2,1)S(1)} %get-tuple-element.156) | copy-start | bytes 1179652 | tf_op jit(solution)/shard_map/cond
  537.5 111.8 %reduce-scatter.26.cloned.1.call-start = ((), (), s32[]{:S(2)}) async-start(), calls=%async_computation.17 | async-start | bytes 417792
  539.9 178.5 %reduce-scatter.22.cloned.1.call-start = ((), (), s32[]{:S(2)}) async-start(), calls=%async_computation.15 | async-start | bytes 3342336
  549.7 235.0 %reduce-scatter.16.cloned.1.call-start = ((), (), s32[]{:S(2)}) async-start(), calls=%async_computation.12 | async-start | bytes 2506752 | tf_op jit(solution)/shard_map/reduce_scatter | solution.py:370
  553.7 325.1 %reduce-scatter.14.cloned.1.call-start = ((), (), s32[]{:S(2)}) async-start(), calls=%async_computation.11 | async-start | bytes 7520256 | tf_op jit(solution)/shard_map/reduce_scatter | solution.py:369
  563.0 431.3 %reduce-scatter.18.cloned.1.call-start = ((), (), s32[]{:S(2)}) async-start(), calls=%async_computation.13 | async-start | bytes 10027008 | tf_op jit(solution)/shard_map/reduce_scatter | solution.py:371
  574.7 536.0 %reduce-scatter.20.cloned.1.call-start = ((), (), s32[]{:S(2)}) async-start(), calls=%async_computation.14 | async-start | bytes 10027008 | tf_op jit(solution)/shard_map/reduce_scatter | solution.py:372
  (85 other events, 326.0 us)
Sparse Core Ops, SparseCore 0:
  10.3 42.7 all-gather.6
  55.4 45.8 all-gather.4
  103.5 52.3 all-gather.8
  158.1 51.9 all-gather.10
  537.6 53.2 reduce-scatter.23
  594.6 54.5 reduce-scatter.25
  653.1 65.2 reduce-scatter.21
  722.7 61.9 reduce-scatter.15
  789.8 89.0 reduce-scatter.13
  883.4 110.8 reduce-scatter.17
  999.6 111.0 reduce-scatter.19
where the time goes:
time: 1130 us; the launch traced here: 1120 us
  waiting for transfers between devices  764 us (68%)
  matrix products  147 us (13%)
  blocking collectives  62.9 us (6%)
  other arithmetic  62.2 us (6%)
  local copies, waits for them, and re-layouts  51.8 us (5%)
  between operations  15.4 us (1%)
    unnamed x14, waiting for transfers between devices  129 us
    reduce_scatter x1, waiting for transfers between devices, body(): lax.psum_scatter(ffn_summed[1][None], 'batch', scatter_dimension=1, tiled...  116 us
    reduce_scatter x1, waiting for transfers between devices, body(): lax.psum_scatter(ffn_summed[0][None], 'batch', scatter_dimension=1, tiled...  115 us
    ppermute x4, waiting for transfers between devices, from_behind(): lax.ppermute(value, axis, [(source, source + steps) for source in range(f...  113 us
    reduce_scatter x1, waiting for transfers between devices, body(): lax.psum_scatter(attn_mats[0][None], 'batch', scatter_dimension=1, tiled=...  94.2 us
    reduce_scatter x1, waiting for transfers between devices, body(): lax.psum_scatter(attn_mats[1][None], 'batch', scatter_dimension=1, tiled=...  64.7 us
    all_gather x1, waiting for transfers between devices, body(): lax.all_gather(up_weight, 'batch', axis=1, tiled=True)  54.7 us
    all_gather x1, waiting for transfers between devices, body(): lax.all_gather(down_weight, 'batch', axis=1, tiled=True)  54.1 us
  transfers between devices with their start and end apart: 15, of which 14 were waited for; matrix products, arithmetic and copies ran while one was open for 6% of the time, Pallas kernels for 0%

commit v1 on v0

v1 whole, which is shorter than its diff:
```python
from functools import partial

import jax
import jax.numpy as jnp
from jax import lax
from jax.experimental import pallas as pl
from jax.experimental.pallas import tpu as pltpu
from jax.sharding import PartitionSpec as P

D = 768
HEADS = 12
FF = 3072
HEAD_DIM = 64
ROW = 256
PAIRS = HEADS // 2
PAIR = 2 * HEAD_DIM
FFC = FF // D
BIAS = 6144
VMEM_LIMIT = 56 * 1024 * 1024

BF = jnp.bfloat16
F32 = jnp.float32
epsilon = 1e-12
masked_value = -1e30
inv_sqrt2 = 0.7071067811865476
inv_sqrt2pi = 0.3989422804014327


def nn(a, b):
    return jnp.dot(a, b, preferred_element_type=F32)


def nt(a, b):
    return lax.dot_general(a, b, (((1,), (1,)), ((), ())), preferred_element_type=F32)


def tn(a, b):
    return lax.dot_general(a, b, (((0,), (0,)), ((), ())), preferred_element_type=F32)


def head_masks():
    lane = lax.broadcasted_iota(jnp.int32, (1, PAIR), 1)
    low = (lane < HEAD_DIM).astype(F32)
    return (low.astype(BF), (1.0 - low).astype(BF))


def segment_penalty(lengths_ref, micro):
    first = lengths_ref[micro, 0]
    second = first + lengths_ref[micro, 1]
    third = second + lengths_ref[micro, 2]

    def number(axis):
        place = lax.broadcasted_iota(jnp.int32, (ROW, ROW), axis)
        one = jnp.where(place >= first, 1, 0)
        two = jnp.where(place >= second, 1, 0)
        return one + two + jnp.where(place >= third, 1, 0)

    return jnp.where(number(0) == number(1), 0.0, masked_value)


def standardize(values):
    centred = values - jnp.mean(values, axis=-1, keepdims=True)
    spread = jnp.mean(centred * centred, axis=-1, keepdims=True)
    scale = lax.rsqrt(spread + epsilon)
    return centred * scale, scale


def norm_back(grad, unit, scale, gain):
    scaled = grad * gain
    mean_one = jnp.mean(scaled, axis=-1, keepdims=True)
    mean_two = jnp.mean(scaled * unit, axis=-1, keepdims=True)
    return scale * (scaled - mean_one - unit * mean_two)


class Copies:
    def __init__(self, sems):
        self.sems = sems
        self.used = 0

    def start(self, src, dst):
        copy = pltpu.make_async_copy(src, dst, self.sems.at[self.used])
        self.used += 1
        copy.start()
        return copy


def chunk(index):
    return slice(index * D, (index + 1) * D)


STATE = (
    ("qkv", (ROW, 3 * D), BF),
    ("probs", (HEADS, ROW, ROW), BF),
    ("context", (ROW, D), BF),
    ("hidden", (ROW, D), BF),
    ("active", (ROW, FF), BF),
    ("slope", (ROW, FF), BF),
    ("unit1", (ROW, D), F32),
    ("unit2", (ROW, D), F32),
    ("scales", (2, ROW, 128), F32),
)
STATE_AT = {entry[0]: place for place, entry in enumerate(STATE)}


def forward_kernel(step, last, *refs):
    info, lengths, biases, gains, shifts, inputs, received = refs[:7]
    qkv_w, out_w, up_w, down_w = refs[7:11]
    result = refs[11]
    outs = refs[12 : 12 + len(STATE)]
    rest = refs[12 + len(STATE) :]
    tokens_v, result_v = rest[:2]
    kept = rest[2 : 2 + len(STATE)]
    qkv_v, out_v, up_v, down_v, first_sum, second_sum, sems = rest[2 + len(STATE) :]
    section = info[0]
    name = {entry[0]: (kept[place], outs[place]) for place, entry in enumerate(STATE)}

    def work():
        copies = Copies(sems)
        if step == 0:
            tokens_in = copies.start(inputs.at[0, 0], tokens_v)
        elif step == last:
            tokens_in = copies.start(received, tokens_v)
        else:
            tokens_in = pltpu.make_async_copy(received, tokens_v, sems.at[copies.used])
            copies.used += 1

            @pl.when(section == 0)
            def _():
                pltpu.make_async_copy(inputs.at[step, 0], tokens_v, tokens_in_sem).start()

            @pl.when(section != 0)
            def _():
                tokens_in.start()

        qkv_in = [copies.start(qkv_w.at[:, chunk(j)], qkv_v.at[:, chunk(j)]) for j in range(3)]
        out_in = copies.start(out_w, out_v)
        up_in = [copies.start(up_w.at[:, chunk(j)], up_v.at[:, chunk(j)]) for j in range(FFC)]
        down_in = [copies.start(down_w.at[chunk(j)], down_v.at[chunk(j)]) for j in range(FFC)]
        leaving = []

        def leave(key, part=None):
            src, dst = name[key]
            if part is not None:
                src, dst = src.at[part], dst.at[part]
            leaving.append(copies.start(src, dst))

        bias = lambda start, size: biases[:, start : start + size].astype(F32)
        penalty = segment_penalty(lengths, jnp.where(section == 0, step, step - 1))
        qkv = name["qkv"][0]
        probs = name["probs"][0]
        tokens_in.wait()
        tokens = tokens_v[...]
        for j in range(3):
            qkv_in[j].wait()
            part = nn(tokens, qkv_v[:, chunk(j)])
            if j != 1:
                part = part + bias(0 if j == 0 else D, D)
            qkv[:, chunk(j)] = part.astype(BF)
        leave("qkv")
        masks = head_masks()
        context = name["context"][0]
        for pair in range(PAIRS):
            at = pair * PAIR
            queries = qkv[:, at : at + PAIR]
            keys = qkv[:, D + at : D + at + PAIR]
            values = qkv[:, 2 * D + at : 2 * D + at + PAIR]
            total = None
            for half in range(2):
                scores = nt(queries * masks[half], keys) * HEAD_DIM ** (-0.5) + penalty
                raised = jnp.exp(scores - jnp.max(scores, axis=-1, keepdims=True))
                share = (raised * (1.0 / jnp.sum(raised, axis=-1, keepdims=True))).astype(BF)
                probs[2 * pair + half] = share
                term = nn(share, values * masks[half])
                total = term if total is None else total + term
            context[:, at : at + PAIR] = total.astype(BF)
            leave("probs", slice(2 * pair, 2 * pair + 2))
        leave("context")
        out_in.wait()
        attended = nn(context[...], out_v[...]) + bias(2 * D, D)
        unit, scale = standardize(tokens.astype(F32) + attended)
        name["unit1"][0][...] = unit
        name["scales"][0][0] = jnp.broadcast_to(scale, (ROW, 128))
        leave("unit1")
        normed = unit * gains[0:1, :] + shifts[0:1, :]
        hidden = name["hidden"][0]
        hidden[...] = normed.astype(BF)
        leave("hidden")
        second_sum[...] = normed + bias(3 * D + FF, D)
        active, slope = name["active"][0], name["slope"][0]
        for j in range(FFC):
            up_in[j].wait()
            inner = nn(hidden[...], up_v[:, chunk(j)]) + bias(3 * D + j * D, D)
            phi = 0.5 * (1.0 + lax.erf(inner * inv_sqrt2))
            active[:, chunk(j)] = (inner * phi).astype(BF)
            bell = jnp.exp(inner * inner * -0.5) * inv_sqrt2pi
            slope[:, chunk(j)] = (phi + inner * bell).astype(BF)
            down_in[j].wait()
            second_sum[...] += nn(active[:, chunk(j)], down_v[chunk(j)])
        leave("active")
        leave("slope")
        unit, scale = standardize(second_sum[...])
        result_v[...] = (unit * gains[1:2, :] + shifts[1:2, :]).astype(BF)
        leaving.append(copies.start(result_v, result))
        name["unit2"][0][...] = unit
        name["scales"][0][1] = jnp.broadcast_to(scale, (ROW, 128))
        leave("unit2")
        leave("scales")
        for copy in leaving:
            copy.wait()

    tokens_in_sem = sems.at[0]
    if step == 0:
        pl.when(section == 0)(work)
    elif step == last:
        pl.when(section != 0)(work)
    else:
        work()


ANY = pl.BlockSpec(memory_space=pl.ANY)
SMEM = pl.BlockSpec(memory_space=pltpu.SMEM)
VMEM = pl.BlockSpec(memory_space=pltpu.VMEM)


def forward(step, last, section, lengths, small, inputs, received, weights):
    biases, gains, shifts = small
    scratch = [pltpu.VMEM((ROW, D), BF), pltpu.VMEM((ROW, D), BF)]
    scratch += [pltpu.VMEM(shape, kind) for _, shape, kind in STATE]
    scratch += [
        pltpu.VMEM((D, 3 * D), BF),
        pltpu.VMEM((D, D), BF),
        pltpu.VMEM((D, FF), BF),
        pltpu.VMEM((FF, D), BF),
        pltpu.VMEM((8, 128), F32),
        pltpu.VMEM((ROW, D), F32),
        pltpu.SemaphoreType.DMA((40,)),
    ]
    outs = pl.pallas_call(
        partial(forward_kernel, step, last),
        out_shape=[jax.ShapeDtypeStruct((ROW, D), BF)]
        + [jax.ShapeDtypeStruct(shape, kind) for _, shape, kind in STATE],
        in_specs=[SMEM, SMEM, VMEM, VMEM, VMEM] + [ANY] * 6,
        out_specs=[ANY] * (1 + len(STATE)),
        scratch_shapes=scratch,
        name="layer_forward",
        compiler_params=pltpu.CompilerParams(vmem_limit_bytes=VMEM_LIMIT),
        cost_estimate=pl.CostEstimate(
            flops=2 * ROW * (12 * D * D), bytes_accessed=24 << 20, transcendentals=ROW * FF
        ),
    )(section, lengths, biases, gains, shifts, inputs, received, *weights)
    return outs[0], outs[1:]


BACK = (
    ("down_side", (ROW, D), BF),
    ("inner", (ROW, FF), BF),
    ("attended", (ROW, D), BF),
    ("joined", (ROW, 3 * D), BF),
    ("norms", (8, D), F32),
)


def backward_kernel(step, last, *refs):
    info, biases, gains, cotangent, received = refs[:5]
    qkv_w, out_w, up_w, down_w = refs[5:9]
    state = refs[9 : 9 + len(STATE)]
    refs = refs[9 + len(STATE) :]
    result = refs[0]
    outs = refs[1 : 1 + len(BACK)]
    refs = refs[1 + len(BACK) :]
    grad_v, result_v, sum_v = refs[:3]
    refs = refs[3:]
    kept = refs[: len(BACK)]
    refs = refs[len(BACK) :]
    qkv_s, probs_s, slope_s, unit1_s, unit2_s, scales_s = refs[:6]
    qkv_v, out_v, up_v, down_v, sems = refs[6:]
    section = info[0]
    name = {entry[0]: (kept[place], outs[place]) for place, entry in enumerate(BACK)}
    held = lambda key: state[STATE_AT[key]]

    def work():
        copies = Copies(sems)
        if step == 0:
            grad_in = copies.start(cotangent.at[last - 1, 0], grad_v)
        elif step == last:
            grad_in = copies.start(received, grad_v)
        else:
            grad_in = pltpu.make_async_copy(received, grad_v, sems.at[0])
            copies.used += 1

            @pl.when(section != 0)
            def _():
                pltpu.make_async_copy(cotangent.at[last - 1 - step, 0], grad_v, sems.at[0]).start()

            @pl.when(section == 0)
            def _():
                grad_in.start()

        unit2_in = copies.start(held("unit2"), unit2_s)
        scales_in = copies.start(held("scales"), scales_s)
        down_in, slope_in, up_in = [], [], []
        for j in range(FFC):
            down_in.append(copies.start(down_w.at[chunk(j)], down_v.at[chunk(j)]))
            slope_in.append(copies.start(held("slope").at[:, chunk(j)], slope_s.at[:, chunk(j)]))
            up_in.append(copies.start(up_w.at[:, chunk(j)], up_v.at[:, chunk(j)]))
        unit1_in = copies.start(held("unit1"), unit1_s)
        out_in = copies.start(out_w, out_v)
        state_in = copies.start(held("qkv"), qkv_s)
        probs_in = copies.start(held("probs"), probs_s)
        qkv_in = copies.start(qkv_w, qkv_v)
        leaving = []

        def leave(key):
            leaving.append(copies.start(*name[key]))

        norms = name["norms"][0]
        grad_in.wait()
        unit2_in.wait()
        scales_in.wait()
        grad = grad_v[...].astype(F32)
        unit = unit2_s[...]
        norms[1:2, :] = jnp.sum(grad * unit, axis=0, keepdims=True)
        norms[3:4, :] = jnp.sum(grad, axis=0, keepdims=True)
        grad = norm_back(grad, unit, scales_s[1, :, 0:1], gains[1:2, :])
        down_side = name["down_side"][0]
        down_side[...] = grad.astype(BF)
        leave("down_side")
        sum_v[...] = grad
        inner = name["inner"][0]
        for j in range(FFC):
            down_in[j].wait()
            through = nt(down_side[...], down_v[chunk(j)])
            slope_in[j].wait()
            inner[:, chunk(j)] = (through * slope_s[:, chunk(j)].astype(F32)).astype(BF)
            up_in[j].wait()
            sum_v[...] += nt(inner[:, chunk(j)], up_v[:, chunk(j)])
        leave("inner")
        grad = sum_v[...]
        unit1_in.wait()
        unit = unit1_s[...]
        norms[0:1, :] = jnp.sum(grad * unit, axis=0, keepdims=True)
        norms[2:3, :] = jnp.sum(grad, axis=0, keepdims=True)
        norms[4:8, :] = jnp.zeros((4, D), F32)
        leave("norms")
        grad = norm_back(grad, unit, scales_s[0, :, 0:1], gains[0:1, :])
        sum_v[...] = grad
        attended = name["attended"][0]
        attended[...] = grad.astype(BF)
        leave("attended")
        out_in.wait()
        context_grad = nt(attended[...], out_v[...]).astype(BF)
        state_in.wait()
        probs_in.wait()
        masks = head_masks()
        joined = name["joined"][0]
        for pair in range(PAIRS):
            at = pair * PAIR
            queries = qkv_s[:, at : at + PAIR]
            keys = qkv_s[:, D + at : D + at + PAIR]
            values = qkv_s[:, 2 * D + at : 2 * D + at + PAIR]
            pair_grad = context_grad[:, at : at + PAIR]
            totals = [None, None, None]
            for half in range(2):
                mask = masks[half]
                share = probs_s[2 * pair + half]
                own_grad = pair_grad * mask
                prob_grad = nt(own_grad, values)
                wide = share.astype(F32)
                weighted = wide * prob_grad
                inner_sum = jnp.sum(weighted, axis=-1, keepdims=True)
                score_grad = ((weighted - wide * inner_sum) * HEAD_DIM ** (-0.5)).astype(BF)
                terms = (
                    nn(score_grad, keys * mask),
                    tn(score_grad, queries * mask),
                    tn(share, own_grad),
                )
                totals = [t if s is None else s + t for s, t in zip(totals, terms)]
            for which in range(3):
                joined[:, which * D + at : which * D + at + PAIR] = totals[which].astype(BF)
        leave("joined")
        qkv_in.wait()
        result_v[...] = (sum_v[...] + nt(joined[...], qkv_v[...])).astype(BF)
        leaving.append(copies.start(result_v, result))
        for copy in leaving:
            copy.wait()

    if step == 0:
        pl.when(section != 0)(work)
    elif step == last:
        pl.when(section == 0)(work)
    else:
        work()


def backward(step, last, section, small, cotangent, received, weights, state):
    biases, gains, shifts = small
    scratch = [pltpu.VMEM((ROW, D), BF), pltpu.VMEM((ROW, D), BF), pltpu.VMEM((ROW, D), F32)]
    scratch += [pltpu.VMEM(shape, kind) for _, shape, kind in BACK]
    scratch += [
        pltpu.VMEM(STATE[STATE_AT[key]][1], STATE[STATE_AT[key]][2])
        for key in ("qkv", "probs", "slope", "unit1", "unit2", "scales")
    ]
    scratch += [
        pltpu.VMEM((D, 3 * D), BF),
        pltpu.VMEM((D, D), BF),
        pltpu.VMEM((D, FF), BF),
        pltpu.VMEM((FF, D), BF),
        pltpu.SemaphoreType.DMA((40,)),
    ]
    outs = pl.pallas_call(
        partial(backward_kernel, step, last),
        out_shape=[jax.ShapeDtypeStruct((ROW, D), BF)]
        + [jax.ShapeDtypeStruct(shape, kind) for _, shape, kind in BACK],
        in_specs=[SMEM, VMEM, VMEM] + [ANY] * (6 + len(STATE)),
        out_specs=[ANY] * (1 + len(BACK)),
        scratch_shapes=scratch,
        name="layer_backward",
        compiler_params=pltpu.CompilerParams(vmem_limit_bytes=VMEM_LIMIT),
        cost_estimate=pl.CostEstimate(
            flops=2 * ROW * (12 * D * D), bytes_accessed=24 << 20, transcendentals=0
        ),
    )(section, biases, gains, cotangent, received, *weights, *state)
    return outs[0], outs[1:]


def two_rows(section, pieces, scratch, copies):
    shared, alone_first, alone_second = pieces
    one = copies.start(shared, scratch.at[0])
    two = pltpu.make_async_copy(alone_first, scratch.at[1], copies.sems.at[copies.used])
    copies.used += 1

    @pl.when(section == 0)
    def _():
        two.start()

    @pl.when(section != 0)
    def _():
        pltpu.make_async_copy(alone_second, scratch.at[1], two_sem(copies)).start()

    return (one, two)


def two_sem(copies):
    return copies.sems.at[copies.used - 1]


def both(ref, columns=slice(None)):
    wide = ref[:, :, columns]
    return wide.reshape(2 * ROW, wide.shape[-1])


def column_sums(values):
    return nn(jnp.ones((8, 2 * ROW), BF), values)[0:1, :]


def ffn_weight_kernel(*refs):
    info = refs[0]
    hidden, active, inner, down_side = (refs[1 + 3 * k : 4 + 3 * k] for k in range(4))
    up_o, down_o, bias_o = refs[13:16]
    hidden_v, active_v, inner_v, down_side_v, up_v, down_v, bias_v, sems = refs[16:]
    section = info[0]
    copies = Copies(sems)
    down_in = two_rows(section, down_side, down_side_v, copies)
    active_in = two_rows(section, active, active_v, copies)
    hidden_in = two_rows(section, hidden, hidden_v, copies)
    inner_in = two_rows(section, inner, inner_v, copies)
    leaving = []
    for copy in down_in + active_in:
        copy.wait()
    down_side_all = both(down_side_v)
    bias_v[:, FF:] = column_sums(down_side_all)
    for j in range(FFC):
        down_v[chunk(j)] = tn(both(active_v, chunk(j)), down_side_all).astype(BF)
        leaving.append(copies.start(down_v.at[chunk(j)], down_o.at[chunk(j)]))
    for copy in hidden_in + inner_in:
        copy.wait()
    hidden_all = both(hidden_v)
    for j in range(FFC):
        inner_part = both(inner_v, chunk(j))
        bias_v[:, chunk(j)] = column_sums(inner_part)
        up_v[:, chunk(j)] = tn(hidden_all, inner_part).astype(BF)
        leaving.append(copies.start(up_v.at[:, chunk(j)], up_o.at[:, chunk(j)]))
    leaving.append(copies.start(bias_v, bias_o))
    for copy in leaving:
        copy.wait()


def ffn_weight(section, hidden, active, inner, down_side):
    return pl.pallas_call(
        ffn_weight_kernel,
        out_shape=[
            jax.ShapeDtypeStruct((D, FF), BF),
            jax.ShapeDtypeStruct((FF, D), BF),
            jax.ShapeDtypeStruct((1, FF + D), F32),
        ],
        in_specs=[SMEM] + [ANY] * 12,
        out_specs=[ANY] * 3,
        scratch_shapes=[
            pltpu.VMEM((2, ROW, D), BF),
            pltpu.VMEM((2, ROW, FF), BF),
            pltpu.VMEM((2, ROW, FF), BF),
            pltpu.VMEM((2, ROW, D), BF),
            pltpu.VMEM((D, FF), BF),
            pltpu.VMEM((FF, D), BF),
            pltpu.VMEM((1, FF + D), F32),
            pltpu.SemaphoreType.DMA((24,)),
        ],
        name="ffn_weights",
        compiler_params=pltpu.CompilerParams(vmem_limit_bytes=VMEM_LIMIT),
        cost_estimate=pl.CostEstimate(
            flops=4 * ROW * (8 * D * D), bytes_accessed=24 << 20, transcendentals=0
        ),
    )(section, *hidden, *active, *inner, *down_side)


def attention_weight_kernel(*refs):
    info = refs[0]
    context, joined, attended, norms = (refs[1 + 3 * k : 4 + 3 * k] for k in range(4))
    inputs, received_one, received_two = refs[13:16]
    qkv_o, out_o, bias_o, norms_o = refs[16:20]
    tokens_v, context_v, joined_v, attended_v, norms_v, qkv_v, out_v, bias_v, sums_v, sems = refs[20:]
    section = info[0]
    copies = Copies(sems)
    attended_in = two_rows(section, attended, attended_v, copies)
    context_in = two_rows(section, context, context_v, copies)
    tokens_sems = [sems.at[copies.used], sems.at[copies.used + 1]]
    copies.used += 2

    @pl.when(section == 0)
    def _():
        pltpu.make_async_copy(inputs.at[1, 0], tokens_v.at[0], tokens_sems[0]).start()
        pltpu.make_async_copy(inputs.at[0, 0], tokens_v.at[1], tokens_sems[1]).start()

    @pl.when(section != 0)
    def _():
        pltpu.make_async_copy(received_one, tokens_v.at[0], tokens_sems[0]).start()
        pltpu.make_async_copy(received_two, tokens_v.at[1], tokens_sems[1]).start()

    tokens_in = (
        pltpu.make_async_copy(received_one, tokens_v.at[0], tokens_sems[0]),
        pltpu.make_async_copy(received_two, tokens_v.at[1], tokens_sems[1]),
    )
    joined_in = two_rows(section, joined, joined_v, copies)
    norms_in = two_rows(section, norms, norms_v, copies)
    leaving = []
    for copy in attended_in + context_in:
        copy.wait()
    attended_all = both(attended_v)
    bias_v[:, 2 * D :] = column_sums(attended_all)
    out_v[...] = tn(both(context_v), attended_all).astype(BF)
    leaving.append(copies.start(out_v, out_o))
    for copy in tokens_in + joined_in:
        copy.wait()
    tokens_all = both(tokens_v)
    for j in range(3):
        joined_part = both(joined_v, chunk(j))
        if j != 1:
            bias_v[:, chunk(j // 2)] = column_sums(joined_part)
        qkv_v[:, chunk(j)] = tn(tokens_all, joined_part).astype(BF)
        leaving.append(copies.start(qkv_v.at[:, chunk(j)], qkv_o.at[:, chunk(j)]))
    leaving.append(copies.start(bias_v, bias_o))
    for copy in norms_in:
        copy.wait()
    sums_v[...] = norms_v[0] + norms_v[1]
    leaving.append(copies.start(sums_v, norms_o))
    for copy in leaving:
        copy.wait()


def attention_weight(section, context, joined, attended, norms, tokens):
    return pl.pallas_call(
        attention_weight_kernel,
        out_shape=[
            jax.ShapeDtypeStruct((D, 3 * D), BF),
            jax.ShapeDtypeStruct((D, D), BF),
            jax.ShapeDtypeStruct((1, 3 * D), F32),
            jax.ShapeDtypeStruct((8, D), F32),
        ],
        in_specs=[SMEM] + [ANY] * 15,
        out_specs=[ANY] * 4,
        scratch_shapes=[
            pltpu.VMEM((2, ROW, D), BF),
            pltpu.VMEM((2, ROW, D), BF),
            pltpu.VMEM((2, ROW, 3 * D), BF),
            pltpu.VMEM((2, ROW, D), BF),
            pltpu.VMEM((2, 8, D), F32),
            pltpu.VMEM((D, 3 * D), BF),
            pltpu.VMEM((D, D), BF),
            pltpu.VMEM((1, 3 * D), F32),
            pltpu.VMEM((8, D), F32),
            pltpu.SemaphoreType.DMA((24,)),
        ],
        name="attention_weights",
        compiler_params=pltpu.CompilerParams(vmem_limit_bytes=VMEM_LIMIT),
        cost_estimate=pl.CostEstimate(
            flops=4 * ROW * (4 * D * D), bytes_accessed=16 << 20, transcendentals=0
        ),
    )(section, *context, *joined, *attended, *norms, *tokens)


def relay(value, steps):
    count = lax.axis_size("section")
    first, last = (max(0, -steps), min(count, count - steps))
    return lax.ppermute(
        value, "section", [(source, source + steps) for source in range(first, last)]
    )


def body(
    inputs,
    cotangent,
    lengths,
    qkv_weight,
    out_weight,
    up_weight,
    down_weight,
    biases,
    norm_gains,
    norm_shifts,
):
    shards = lax.axis_size("batch")
    width = D // shards
    bias_width = BIAS // shards
    place = lax.axis_index("section")
    section = place.astype(jnp.int32).reshape(1)
    first_section = place == 0
    gather = lambda value: lax.all_gather(value, "batch", axis=0, tiled=True)
    packed = jnp.concatenate([biases[0], norm_gains[0].reshape(-1), norm_shifts[0].reshape(-1)])
    small_all = gather(packed[None])
    weights = (
        gather(qkv_weight[0]),
        gather(out_weight[0]),
        gather(up_weight[0]),
        gather(down_weight[0]),
    )
    unpack = lambda start: (
        small_all[:, start : start + 2 * width]
        .reshape(shards, 2, width)
        .transpose(1, 0, 2)
        .reshape(2, D)
        .astype(F32)
    )
    small = (
        small_all[:, :bias_width].reshape(1, BIAS),
        unpack(bias_width),
        unpack(bias_width + 2 * width),
    )
    lengths = lengths[:, 0]
    micro_count = inputs.shape[0]
    last = micro_count
    received = inputs[0, 0]
    results, states, arrivals = [], [], []
    for step in range(last + 1):
        result, state = forward(
            step, last, section, lengths, small, inputs, received, weights
        )
        results.append(result)
        states.append(state)
        arrivals.append(received)
        if step < last:
            received = relay(result, 1)
    received = cotangent[0, 0]
    grads, backs = [], []
    for step in range(last + 1):
        grad, back = backward(
            step, last, section, small, cotangent, received, weights, states[last - step]
        )
        grads.append(grad)
        backs.append(back)
        if step < last:
            received = relay(grad, -1)
    rows = lambda key: (states[1][STATE_AT[key]], states[0][STATE_AT[key]], states[2][STATE_AT[key]])
    turns = lambda at: (backs[1][at], backs[2][at], backs[0][at])
    up_mat, down_mat, ffn_bias = ffn_weight(
        section, rows("hidden"), rows("active"), turns(1), turns(0)
    )
    qkv_mat, out_mat, attn_bias, norms = attention_weight(
        section,
        rows("context"),
        turns(3),
        turns(2),
        turns(4),
        (inputs, arrivals[1], arrivals[2]),
    )
    scatter = lambda value: lax.psum_scatter(value, "batch", scatter_dimension=0, tiled=True)
    bias_total = jnp.concatenate([attn_bias[0], ffn_bias[0]]).reshape(shards, bias_width)
    norm_total = norms[:4].reshape(4, shards, width).transpose(1, 0, 2).reshape(shards, 4 * width)
    small_total = jnp.concatenate([bias_total, norm_total], axis=1)
    up_sum = scatter(up_mat).astype(F32)[None]
    down_sum = scatter(down_mat).astype(F32)[None]
    qkv_sum = scatter(qkv_mat).astype(F32)[None]
    out_sum = scatter(out_mat).astype(F32)[None]
    small_sum = scatter(small_total)
    norm_sum = small_sum[:, bias_width:].reshape(1, 4, width)
    activations = jnp.stack(
        [jnp.where(first_section, results[m], results[m + 1]) for m in range(micro_count)]
    )[None, :, None]
    input_grads = jnp.stack(
        [
            jnp.where(first_section, grads[micro_count - m], grads[micro_count - 1 - m])
            for m in range(micro_count)
        ]
    )[None, :, None]
    return (
        activations,
        input_grads,
        qkv_sum,
        out_sum,
        up_sum,
        down_sum,
        small_sum[:, :bias_width],
        norm_sum[:, :2],
        norm_sum[:, 2:],
    )


def solution(mesh):
    in_specs = (
        P(None, "batch", None, None),
        P(None, "batch", None, None),
        P(None, "batch", None),
        P("section", "batch", None),
        P("section", "batch", None),
        P("section", "batch", None),
        P("section", "batch", None),
        P("section", "batch"),
        P("section", None, "batch"),
        P("section", None, "batch"),
    )
    out_specs = (
        P("section", None, "batch", None, None),
        P("section", None, "batch", None, None),
        P("section", "batch", None),
        P("section", "batch", None),
        P("section", "batch", None),
        P("section", "batch", None),
        P("section", "batch"),
        P("section", None, "batch"),
        P("section", None, "batch"),
    )
    return jax.shard_map(body, mesh=mesh, in_specs=in_specs, out_specs=out_specs, check_vma=False)
```

time: 1130 us -> 652 us (0.58)
  waiting for transfers between devices: 764 us -> 390 us
  matrix products: 147 us -> 0 us
  Pallas kernels: 0 us -> 80.3 us
  blocking collectives: 62.9 us -> 121 us
  other arithmetic: 62.2 us -> 9.26 us
  local copies, waits for them, and re-layouts: 51.8 us -> 14.4 us
    reduce_scatter x4, waiting for transfers between devices: 391 us -> 205 us  [body(): lax.psum_scatter(value, 'batch', scatter_dimension=0, tiled=True)]
    dot_general x41 -> x0, matrix products: 147 us -> none  [the longest x2 15.3 us: layer_forward(): jnp.dot(hidden, up_w, preferred_element_type=jnp.float32)]
    unnamed x14 -> x8, waiting for transfers between devices: 129 us -> 3.8 us
    unnamed x0 -> x2, blocking collectives: none -> 121 us
    pallas_call x0 -> x8, Pallas kernels: none -> 80.3 us  [the longest x3 35.2 us: backward(): pl.pallas_call(partial(backward_kernel, step, last), out_shape=[jax.Shape...]
    all_gather x3 -> x0, blocking collectives: 62.9 us -> none  [the longest x1 25 us: body(): lax.all_gather(norm_gains, 'batch', axis=2, tiled=True)]
    ppermute x4, waiting for transfers between devices: 113 us -> 54.4 us  [relay(): lax.ppermute(value, 'section', [(source, source + steps) for source in ra...]
    reduce_sum x24 -> x0, other arithmetic: 26.1 us -> none  [the longest x5 7.58 us: layer_norm(): return centred * lax.rsqrt(spread + epsilon) * gain_vec + shift_vec]
  transfers between devices with their start and end apart: 15 -> 12, of which waited for: 14 -> 10; matrix products, arithmetic and copies ran while one was open for 6% -> 3% of each run, Pallas kernels for 0% -> 1%
where the time goes in v1:
time: 652 us; the launch traced here: 644 us
  waiting for transfers between devices  390 us (60%)
  blocking collectives  121 us (19%)
  Pallas kernels  80.3 us (12%)
  between operations  15.5 us (2%)
  local copies, waits for them, and re-layouts  14.4 us (2%)
  starting transfers between devices  13.6 us (2%)
  other arithmetic  9.26 us (1%)
    reduce_scatter x4, waiting for transfers between devices, body(): lax.psum_scatter(value, 'batch', scatter_dimension=0, tiled=True)  205 us
    all_gather x4, waiting for transfers between devices, body(): gather = lambda value: lax.all_gather(value, 'batch', axis=0, tiled=True)  127 us
    unnamed x2, blocking collectives  121 us
    ppermute x4, waiting for transfers between devices, relay(): lax.ppermute(value, 'section', [(source, source + steps) for source in ra...  54.4 us
    pallas_call x3, Pallas kernels, backward(): pl.pallas_call(partial(backward_kernel, step, last), out_shape=[jax.Shape...  35.2 us
    pallas_call x3, Pallas kernels, forward(): pl.pallas_call(partial(forward_kernel, step, last), out_shape=[jax.ShapeD...  29.6 us
    ppermute x4, starting transfers between devices, relay(): lax.ppermute(value, 'section', [(source, source + steps) for source in ra...  13.1 us
  transfers between devices with their start and end apart: 12, of which 10 were waited for; matrix products, arithmetic and copies ran while one was open for 3% of the time, Pallas kernels for 1%

profile of v1, /device:TPU:0, one launch (start us, length us, event | category | flops | bytes accessed | tf_op | source)
XLA Modules:
  0.0 643.9 jit_solution(4937121177989732347)
XLA Ops:
  12.2 1.3 fusion.1
  14.5 63.3 %all-reduce = bf16[9216]{0:T(1024)(128)(2,1)S(1)} all-reduce(bf16[9216]{0:T(1024)(128)(2,1)S(1)} %dynamic-update-slice), channel_id=2, replica_groups=mesh['section'=2,'batch'=16] {'batch'}, use_global_device_ids=true, to_apply=%add | all-reduce | flops 9216 | bytes 36864
  80.1 1.8 slice_bitcast_fusion.1.refs_6_
  81.8 17.9 %all-gather.10.cloned.1.call-done = bf16[1,768,2304]{2,1,0:T(8,128)(2,1)} async-done(((bf16[1,48,2304]{2,1,0:T(8,128)(2,1)}), bf16[1,768,2304]{2,1,0:T(8,128)(2,1)}) %all-gather.10.cloned.1.call-update) | async-done | bytes 3538960 | tf_op jit(solution)/shard_map/all_gather | solution.py:627
  99.7 54.7 %all-gather.14.cloned.1.call-done = bf16[1,768,3072]{2,1,0:T(8,128)(2,1)} async-done(((bf16[1,48,3072]{2,1,0:T(8,128)(2,1)}), bf16[1,768,3072]{2,1,0:T(8,128)(2,1)}) %all-gather.14.cloned.1.call-update) | async-done | bytes 4718608 | tf_op jit(solution)/shard_map/all_gather | solution.py:627
  154.5 54.1 %all-gather.16.cloned.1.call-done = bf16[1,3072,768]{2,1,0:T(8,128)(2,1)} async-done(((bf16[1,192,768]{2,1,0:T(8,128)(2,1)}), bf16[1,3072,768]{2,1,0:T(8,128)(2,1)}) %all-gather.16.cloned.1.call-update) | async-done | bytes 4718608 | tf_op jit(solution)/shard_map/all_gather | solution.py:627
  208.6 14.1 %layer_forward.3 = (bf16[256,768]{1,0:T(8,128)(2,1)}, bf16[256,2304]{1,0:T(8,128)(2,1)}, bf16[12,256,256]{2,1,0:T(8,128)(2,1)}, bf16[256,768]{1,0:T(8,128)(2,1)}...) custom-call(s32[1]{0:T(128)} %bitcast.refs_0_, ...), custom_call_target="tpu_custom_call" | custom-call | flops 3623878656 | bytes 25165824 | tf_op jit(solution)/shard_map/layer_forward/pallas_call | solution.py:238
  222.7 1.7 collective-permute-start
  224.4 9.1 %collective-permute-done.refs_6_.refs_14_ = bf16[256,768]{1,0:T(8,128)(2,1)S(1)} collective-permute-done((bf16[256,768]{1,0:T(8,128)(2,1)}, bf16[256,768]{1,0:T(8,128)(2,1)S(1)}, u32[]{:S(2)}, u32[]{:S(2)}) %collective-permute-start) | collective-permute-done | bytes 393248 | tf_op jit(solution)/shard_map/ppermute | solution.py:604
  234.2 14.1 %layer_forward.4 = (bf16[256,768]{1,0:T(8,128)(2,1)}, bf16[256,2304]{1,0:T(8,128)(2,1)}, bf16[12,256,256]{2,1,0:T(8,128)(2,1)}, bf16[256,768]{1,0:T(8,128)(2,1)}...) custom-call(s32[1]{0:T(128)} %bitcast.refs_0_, ...), custom_call_target="tpu_custom_call" | custom-call | flops 3623878656 | bytes 25165824 | tf_op jit(solution)/shard_map/layer_forward/pallas_call | solution.py:238
  248.3 4.3 collective-permute-start.1
  253.4 7.8 %collective-permute-done.1.refs_6_.refs_15_ = bf16[256,768]{1,0:T(8,128)(2,1)S(1)} collective-permute-done((bf16[256,768]{1,0:T(8,128)(2,1)}, bf16[256,768]{1,0:T(8,128)(2,1)S(1)}, u32[]{:S(2)}, u32[]{:S(2)}) %collective-permute-start.1) | collective-permute-done | bytes 393248 | tf_op jit(solution)/shard_map/ppermute | solution.py:604
  262.0 1.4 layer_forward.5
  263.4 6.4 layer_backward.3
  269.9 5.8 collective-permute-start.2
  275.7 27.4 %collective-permute-done.2.refs_4_ = bf16[256,768]{1,0:T(8,128)(2,1)S(1)} collective-permute-done((bf16[256,768]{1,0:T(8,128)(2,1)}, bf16[256,768]{1,0:T(8,128)(2,1)S(1)}, u32[]{:S(2)}, u32[]{:S(2)}) %collective-permute-start.2) | collective-permute-done | bytes 393248 | tf_op jit(solution)/shard_map/ppermute | solution.py:604
  303.9 14.3 %layer_backward.4 = (bf16[256,768]{1,0:T(8,128)(2,1)}, bf16[256,768]{1,0:T(8,128)(2,1)}, bf16[256,3072]{1,0:T(8,128)(2,1)}, bf16[256,768]{1,0:T(8,128)(2,1)}, bf...) custom-call(s32[1]{0:T(128)} %bitcast.refs_0_, bf16[1,6144]{1,0:T(2,128)(2,1)} %bitcast.77, f32[2,768]{1,0:T(2,128)} %reshape.54.refs_3_.refs_2_, ...), custom_call_target="tpu_custom_call" | custom-call | flops 3623878656 | bytes 25165824 | tf_op jit(solution)/shard_map/layer_backward/pallas_call | solution.py:410
  318.2 1.3 collective-permute-start.3
  319.5 10.1 %collective-permute-done.3.refs_4_ = bf16[256,768]{1,0:T(8,128)(2,1)S(1)} collective-permute-done((bf16[256,768]{1,0:T(8,128)(2,1)}, bf16[256,768]{1,0:T(8,128)(2,1)S(1)}, u32[]{:S(2)}, u32[]{:S(2)}) %collective-permute-start.3) | collective-permute-done | bytes 393248 | tf_op jit(solution)/shard_map/ppermute | solution.py:604
  330.3 14.5 %layer_backward.5 = (bf16[256,768]{1,0:T(8,128)(2,1)}, bf16[256,768]{1,0:T(8,128)(2,1)}, bf16[256,3072]{1,0:T(8,128)(2,1)}, bf16[256,768]{1,0:T(8,128)(2,1)}, bf...) custom-call(s32[1]{0:T(128)} %bitcast.refs_0_, bf16[1,6144]{1,0:T(2,128)(2,1)} %bitcast.78, f32[2,768]{1,0:T(2,128)} %reshape.54.refs_3_.refs_2_, ...), custom_call_target="tpu_custom_call" | custom-call | flops 3623878656 | bytes 25165824 | tf_op jit(solution)/shard_map/layer_backward/pallas_call | solution.py:410
  344.9 5.9 attention_weights.1
  351.7 9.5 %ffn_weights.1 = (bf16[768,3072]{1,0:T(8,128)(2,1)}, bf16[3072,768]{1,0:T(8,128)(2,1)}, f32[1,3840]{1,0:T(1,128)}) custom-call(s32[1]{0:T(128)} %bitcast.refs_0_, bf16[256,768]{1,0:T(8,128)(2,1)} %get-tuple-element.80.refs_12_.refs_1_, bf16[256,768]{1,0:T(8,128)(2,1)} %get-tuple-element.90.refs_12_.refs_2_, ...), custom_call_target="tpu_custom_call" | custom-call | flops 4831838208 | bytes 25165824 | tf_op jit(solution)/shard_map/ffn_weights/pallas_call | solution.py:489
  363.1 57.8 %all-reduce.1 = f32[16,576]{1,0:T(8,128)S(1)} all-reduce(f32[16,576]{1,0:T(8,128)S(1)} %pad_maximum_fusion), channel_id=11, replica_groups=mesh['section'=2,'batch'=16] {'batch'}, use_global_device_ids=true, to_apply=%region_4.0.clone | all-reduce | flops 9216 | bytes 73728
  421.7 1.2 constant_dynamic-slice_fusion
  423.0 1.3 maximum_bitcast_fusion
  424.9 1.6 bitcast_convert_fusion.3
  426.4 51.2 %reduce-scatter.5.cloned.1.call-done = bf16[48,2304]{1,0:T(8,128)(2,1)} async-done(((bf16[768,2304]{1,0:T(8,128)(2,1)}), bf16[48,2304]{1,0:T(8,128)(2,1)}) %reduce-scatter.5.cloned.1.call-update) | async-done | bytes 221200 | tf_op jit(solution)/shard_map/reduce_scatter | solution.py:685
  477.6 1.7 bitcast_convert_fusion.2
  479.3 76.5 %reduce-scatter.9.cloned.1.call-done = bf16[48,3072]{1,0:T(8,128)(2,1)} async-done(((bf16[768,3072]{1,0:T(8,128)(2,1)}), bf16[48,3072]{1,0:T(8,128)(2,1)}) %reduce-scatter.9.cloned.1.call-update) | async-done | bytes 294928 | tf_op jit(solution)/shard_map/reduce_scatter | solution.py:685
  555.8 1.8 bitcast_convert_fusion.1
  557.6 77.2 %reduce-scatter.11.cloned.1.call-done = bf16[192,768]{1,0:T(8,128)(2,1)} async-done(((bf16[3072,768]{1,0:T(8,128)(2,1)}), bf16[192,768]{1,0:T(8,128)(2,1)}) %reduce-scatter.11.cloned.1.call-update) | async-done | bytes 294928 | tf_op jit(solution)/shard_map/reduce_scatter | solution.py:685
  634.9 1.8 bitcast_convert_fusion
  (77 shorter events, 15.5 us)
Async XLA Ops:
  7.2 74.6 %all-gather.12.cloned.1.call-start = ((), (), s32[]{:S(2)}) async-start(), calls=%async_computation.9 | async-start | bytes 1253376 | tf_op jit(solution)/shard_map/all_gather | solution.py:627
  7.9 91.8 %all-gather.10.cloned.1.call-start = ((), (), s32[]{:S(2)}) async-start(), calls=%async_computation.8 | async-start | bytes 3760128 | tf_op jit(solution)/shard_map/all_gather | solution.py:627
  8.7 145.8 %all-gather.14.cloned.1.call-start = ((), (), s32[]{:S(2)}) async-start(), calls=%async_computation.10 | async-start | bytes 5013504 | tf_op jit(solution)/shard_map/all_gather | solution.py:627
  9.4 199.2 %all-gather.16.cloned.1.call-start = ((), (), s32[]{:S(2)}) async-start(), calls=%async_computation.11 | async-start | bytes 5013504 | tf_op jit(solution)/shard_map/all_gather | solution.py:627
  10.0 414.9 %reduce-scatter.7.cloned.1.call-start = ((), (), s32[]{:S(2)}) async-start(), calls=%async_computation.5 | async-start | bytes 1253376 | tf_op jit(solution)/shard_map/reduce_scatter | solution.py:685
  222.7 30.0 %copy-start = (bf16[2,1,256,768]{3,2,1,0:T(8,128)(2,1)S(1)}, bf16[2,1,256,768]{3,2,1,0:T(8,128)(2,1)}, u32[]{:S(2)}) copy-start(bf16[2,1,256,768]{3,2,1,0:T(8,128)(2,1)} %refs_3_.5) | copy-start | bytes 2359300
  222.7 10.8 %collective-permute-start = (bf16[256,768]{1,0:T(8,128)(2,1)}, bf16[256,768]{1,0:T(8,128)(2,1)S(1)}, u32[]{:S(2)}, u32[]{:S(2)}) collective-permute-start(bf16[256,768]{1,0:T(8,128)(2,1)} %get-tuple-element.64), channel_id=1, source_target_pairs={{0,16},{1,17},{2,18},{3,19},{4,20},{5,21},{6,22},{7,23},{8,24},{9,... | collective-permute-start | bytes 1179656 | tf_op jit(solution)/shard_map/ppermute | solution.py:604
  233.5 0.7 copy-start.9
  248.3 12.9 %collective-permute-start.1 = (bf16[256,768]{1,0:T(8,128)(2,1)}, bf16[256,768]{1,0:T(8,128)(2,1)S(1)}, u32[]{:S(2)}, u32[]{:S(2)}) collective-permute-start(bf16[256,768]{1,0:T(8,128)(2,1)} %get-tuple-element.65), channel_id=1, source_target_pairs={{0,16},{1,17},{2,18},{3,19},{4,20},{5,21},{6,22},{7,23},{8,24},{9,... | collective-permute-start | bytes 1179656 | tf_op jit(solution)/shard_map/ppermute | solution.py:604
  261.2 0.8 copy-start.10
  269.9 33.3 %collective-permute-start.2 = (bf16[256,768]{1,0:T(8,128)(2,1)}, bf16[256,768]{1,0:T(8,128)(2,1)S(1)}, u32[]{:S(2)}, u32[]{:S(2)}) collective-permute-start(bf16[256,768]{1,0:T(8,128)(2,1)} %get-tuple-element.76), channel_id=1, source_target_pairs={{16,0},{17,1},{18,2},{19,3},{20,4},{21,5},{22,6},{23,7},{24,8},{25... | collective-permute-start | bytes 1179656 | tf_op jit(solution)/shard_map/ppermute | solution.py:604
  303.1 0.8 copy-start.8
  318.2 11.4 %collective-permute-start.3 = (bf16[256,768]{1,0:T(8,128)(2,1)}, bf16[256,768]{1,0:T(8,128)(2,1)S(1)}, u32[]{:S(2)}, u32[]{:S(2)}) collective-permute-start(bf16[256,768]{1,0:T(8,128)(2,1)} %get-tuple-element.86), channel_id=1, source_target_pairs={{16,0},{17,1},{18,2},{19,3},{20,4},{21,5},{22,6},{23,7},{24,8},{25... | collective-permute-start | bytes 1179656 | tf_op jit(solution)/shard_map/ppermute | solution.py:604
  329.6 0.8 copy-start.7
  350.8 126.8 %reduce-scatter.5.cloned.1.call-start = ((), (), s32[]{:S(2)}) async-start(), calls=%async_computation.4 | async-start | bytes 3760128 | tf_op jit(solution)/shard_map/reduce_scatter | solution.py:685
  351.4 204.4 %reduce-scatter.9.cloned.1.call-start = ((), (), s32[]{:S(2)}) async-start(), calls=%async_computation.6 | async-start | bytes 5013504 | tf_op jit(solution)/shard_map/reduce_scatter | solution.py:685
  361.2 273.6 %reduce-scatter.11.cloned.1.call-start = ((), (), s32[]{:S(2)}) async-start(), calls=%async_computation.7 | async-start | bytes 5013504 | tf_op jit(solution)/shard_map/reduce_scatter | solution.py:685
  361.3 1.0 copy-start.1
  361.3 1.1 copy-start.3
  361.3 1.2 copy-start.5
  362.0 0.8 copy-start.13
  362.0 1.0 copy-start.11
  362.0 1.0 copy-start.12
  362.0 60.9 %copy-start.2 = (bf16[256,768]{1,0:T(8,128)(2,1)S(1)}, bf16[256,768]{1,0:T(8,128)(2,1)}, u32[]{:S(2)}) copy-start(bf16[256,768]{1,0:T(8,128)(2,1)} %get-tuple-element.76) | copy-start | bytes 1179652
  362.0 60.9 %copy-start.4 = (bf16[256,768]{1,0:T(8,128)(2,1)S(1)}, bf16[256,768]{1,0:T(8,128)(2,1)}, u32[]{:S(2)}) copy-start(bf16[256,768]{1,0:T(8,128)(2,1)} %get-tuple-element.86) | copy-start | bytes 1179652
  362.0 60.9 %copy-start.6 = (bf16[256,768]{1,0:T(8,128)(2,1)S(1)}, bf16[256,768]{1,0:T(8,128)(2,1)}, u32[]{:S(2)}) copy-start(bf16[256,768]{1,0:T(8,128)(2,1)} %get-tuple-element.96) | copy-start | bytes 1179652
Sparse Core Ops, SparseCore 0:
  10.3 41.1 all-gather.11
  53.8 45.9 all-gather.9
  102.0 52.3 all-gather.13
  156.6 51.9 all-gather.15
  351.0 55.8 reduce-scatter.6
  410.5 67.0 reduce-scatter.4
  481.5 74.3 reduce-scatter.8
  560.2 74.6 reduce-scatter.10
